TPU v7x, 256 devices: a whole 4x4x8 slice. The times are simulated.
256 devices in a mesh: seq: 32 (over x, y, core), head: 8 (over z).
Axes of the slice: x: 4, y: 4, z: 8, core: 2. Of those that a mesh axis runs over, the one named last changes fastest.
Arguments:
- query_vectors: bfloat16 [32768, 4096], P('seq', 'head'), may hold values from -6 to 6
- key_vectors: bfloat16 [32768, 4096], P('seq', 'head'), may hold values from -6 to 6
- value_vectors: bfloat16 [32768, 4096], P('seq', 'head'), may hold values from -120 to 120
- send_slots: int32 [1024, 48], P('seq'), may hold values from 0 to 1024, as said below
- receive_slots: int32 [1024, 48], P('seq'), may hold values from 0 to 1024, as said below
- resets: int32 [256], P('seq'), may hold values 0 or 1
Outputs:
- attended: bfloat16 [32768, 4096], P('seq', 'head')
Inputs may be any that keep to these rules, and one draw needn't show every extreme that they name: `send_slots`: row s * 32 + d lists in its first slots distinct local rows of device s that go to device d and holds 1024 in the rest; every local row of every device is listed once; no row has more than 48 live slots, and every device sends 48 rows to some device and receives 48 rows from some device. `receive_slots`: row d * 32 + s holds, slot for slot with row s * 32 + d of send_slots, distinct context positions on device d, and 1024 where that slot is empty; every position of every device is named once.
All inputs are finite; a program needn't handle non-finite values. No bound on the sum of `resets` on one device may be relied on, other than what follows from the above.
Results may differ from a plain program's by a relative error of at most 0.0049.
Values may be sent and summed in bfloat16 or wider, within the bound.
A program may use at most 64 MiB of HBM per device.

v0:
```python
import jax
import jax.numpy as jnp
from jax import lax
from jax.sharding import PartitionSpec as P

H = 32
HD = 128
CH = 128


epsilon = 1e-05


def prefix(value, axis, join, neutral):
    count, mine = (lax.axis_size(axis), lax.axis_index(axis))
    pieces = jax.tree.map(lambda part: lax.all_gather(part, axis), value)
    subtotal = jax.tree.map(
        lambda part, zero: jnp.full_like(part, 0) + jnp.asarray(zero, part.dtype), value, neutral
    )

    def lap(position, subtotal):
        longer = join(subtotal, jax.tree.map(lambda part: part[position], pieces))
        return jax.tree.map(lambda new, old: jnp.where(position < mine, new, old), longer, subtotal)

    return lax.fori_loop(0, count - 1, lap, subtotal)


def shards(query_vectors, key_vectors, value_vectors, send_slots, receive_slots, resets):
    tok_count = query_vectors.shape[0]
    row_width = query_vectors.shape[1]
    heads_here = row_width // HD
    group_count = tok_count // CH

    def pack_rows(source_rows, slot_table):
        padded = jnp.concatenate([source_rows, jnp.zeros((1, row_width), source_rows.dtype)], 0)
        return jnp.take(padded, slot_table, axis=0)

    def place_rows(arrived, slot_table):
        flat_rows = arrived.reshape(-1, row_width)
        placed = (
            jnp.zeros((tok_count + 1, row_width), arrived.dtype)
            .at[slot_table.reshape(-1)]
            .set(flat_rows)
        )
        return placed[:tok_count]

    def to_groups(rows_here):
        return rows_here.reshape(group_count, CH, heads_here, HD)

    q_arrived, k_arrived, v_arrived = (
        lax.all_to_all(
            pack_rows(query_vectors, send_slots), "seq", split_axis=0, concat_axis=0, tiled=True
        ),
        lax.all_to_all(
            pack_rows(key_vectors, send_slots), "seq", split_axis=0, concat_axis=0, tiled=True
        ),
        lax.all_to_all(
            pack_rows(value_vectors, send_slots), "seq", split_axis=0, concat_axis=0, tiled=True
        ),
    )
    k_blocks = to_groups(place_rows(k_arrived, receive_slots))
    v_blocks = to_groups(place_rows(v_arrived, receive_slots))
    group_kv = jnp.einsum("cthd,cthe->chde", k_blocks, v_blocks, preferred_element_type=jnp.float32)

    def local_step(carry_pair, group_item):
        carried, seen_reset = carry_pair
        group_state, reset_flag = group_item
        carried = jnp.where(reset_flag > 0, 0.0, carried)
        seen_reset = jnp.maximum(seen_reset, reset_flag)
        return ((carried + group_state, seen_reset), (carried, seen_reset))

    initial = (jnp.zeros((heads_here, HD, HD), jnp.float32), jnp.int32(0))
    (final_state, seen_all), (group_starts, seen_each) = lax.scan(
        local_step, initial, (group_kv, resets)
    )
    reset_mark = seen_all.astype(jnp.float32)

    def combine(earlier, later):
        return (jnp.maximum(earlier[0], later[0]), later[1] + (1.0 - later[0]) * earlier[1])

    identity = (jnp.float32(0.0), jnp.zeros((heads_here, HD, HD), jnp.float32))
    _, carry_in = prefix((reset_mark, final_state), "seq", combine, identity)
    keep_carry = (1 - seen_each).astype(jnp.float32)[:, None, None, None]
    incoming = group_starts + keep_carry * carry_in
    q_blocks = to_groups(place_rows(q_arrived, receive_slots))
    state_rounded = incoming.astype(jnp.bfloat16)
    inter_term = jnp.einsum(
        "cthd,chde->cthe", q_blocks, state_rounded, preferred_element_type=jnp.float32
    )
    scores = jnp.einsum("cthd,cshd->chts", q_blocks, k_blocks, preferred_element_type=jnp.float32)
    causal = jnp.arange(CH)[:, None] >= jnp.arange(CH)[None, :]
    weights = jnp.where(causal[None, None], scores, 0.0).astype(jnp.bfloat16)
    intra_term = jnp.einsum(
        "chts,cshe->cthe", weights, v_blocks, preferred_element_type=jnp.float32
    )
    raw_out = (inter_term + intra_term).reshape(tok_count, row_width)
    row_squares = jnp.sum(raw_out * raw_out, axis=1)
    total_squares = lax.psum(row_squares, "head")
    normed = (raw_out * lax.rsqrt(total_squares / (H * HD) + epsilon)[:, None]).astype(jnp.bfloat16)
    returned = lax.all_to_all(
        pack_rows(normed, receive_slots), "seq", split_axis=0, concat_axis=0, tiled=True
    )
    return place_rows(returned, send_slots)


def solution(mesh):
    placed = (
        P("seq", "head"),
        P("seq", "head"),
        P("seq", "head"),
        P("seq", None),
        P("seq", None),
        P("seq"),
    )
    return jax.shard_map(
        shards, mesh=mesh, in_specs=placed, out_specs=P("seq", "head"), check_vma=False
    )
```

profile of v0, /device:TPU:1, one launch (start us, length us, event | category | flops | bytes accessed | tf_op | source)
XLA Modules:
  0.0 397.4 jit_solution(14778778138887799986)
XLA Ops:
  9.7 5.4 %gather_fusion.2 = bf16[1536,512]{1,0:T(8,128)(2,1)} fusion(bf16[1025,512]{1,0:T(8,128)(2,1)S(1)} %concatenate.14, s32[2048]{0:T(1024)S(1)} %pad_clamp_fusion.1), kind=kCustom, calls=%fused_computation.2.clone | custom fusion | bytes 3151872 | tf_op jit(solution)/shard_map/jit(_take)/gather | solution.py:36
  15.1 5.4 %gather_fusion = bf16[1536,512]{1,0:T(8,128)(2,1)} fusion(bf16[1025,512]{1,0:T(8,128)(2,1)S(1)} %concatenate.12, s32[2048]{0:T(1024)S(1)} %pad_clamp_fusion.1), kind=kCustom, calls=%fused_computation.clone | custom fusion | bytes 3151872 | tf_op jit(solution)/shard_map/jit(_take)/gather | solution.py:36
  20.6 5.4 %gather_fusion.1 = bf16[1536,512]{1,0:T(8,128)(2,1)} fusion(bf16[1025,512]{1,0:T(8,128)(2,1)S(1)} %concatenate.13, s32[2048]{0:T(1024)S(1)} %pad_clamp_fusion.1), kind=kCustom, calls=%fused_computation.1.clone | custom fusion | bytes 3151872 | tf_op jit(solution)/shard_map/jit(_take)/gather | solution.py:36
  26.0 3.8 broadcast_select_fusion.1
  29.8 31.3 %all_to_all.20 = bf16[32,48,512]{2,1,0:T(8,128)(2,1)} all-to-all(bf16[32,48,512]{2,1,0:T(8,128)(2,1)S(1)} %get-tuple-element.212), channel_id=1, replica_groups=mesh['seq'=32,'head'=8] {'seq'}, dimensions={0} | all-to-all | bytes 3145728 | tf_op jit(solution)/shard_map/all_to_all | solution.py:57
  61.1 4.6 %all-to-all-start = ((bf16[32,48,512]{2,1,0:T(8,128)(2,1)}), bf16[32,48,512]{2,1,0:T(8,128)(2,1)}, u32[]{:S(2)}, u32[]{:S(2)}) async-start(bf16[32,48,512]{2,1,0:T(8,128)(2,1)} %get-tuple-element.213), calls=%async_computation | async-start | bytes 3145728 | tf_op jit(solution)/shard_map/all_to_all | solution.py:54
  66.0 8.0 %scatter_custom_fusion.1 = bf16[1025,512]{1,0:T(8,128)(2,1)S(1)} fusion(s32[1536]{0:T(1024)S(1)} %fusion.23, bf16[1536,512]{1,0:T(8,128)(2,1)} %bitcast.60, bf16[]{:T(256)} %constant.68.clone.1), kind=kCustom, calls=%fused_computation.37 | custom fusion | bytes 1050112 | tf_op jit(solution)/shard_map/scatter | solution.py:43
  75.0 13.1 %all-to-all-done = bf16[32,48,512]{2,1,0:T(8,128)(2,1)} async-done(((bf16[32,48,512]{2,1,0:T(8,128)(2,1)}), bf16[32,48,512]{2,1,0:T(8,128)(2,1)}, u32[]{:S(2)}, u32[]{:S(2)}) %all-to-all-start) | async-done | bytes 1572896 | tf_op jit(solution)/shard_map/all_to_all | solution.py:54
  88.2 8.0 %scatter_custom_fusion = bf16[1025,512]{1,0:T(8,128)(2,1)S(1)} fusion(s32[1536]{0:T(1024)S(1)} %fusion.23, bf16[1536,512]{1,0:T(8,128)(2,1)} %bitcast.1, bf16[]{:T(256)} %constant.68.clone.1), kind=kCustom, calls=%fused_computation.39 | custom fusion | bytes 1050112 | tf_op jit(solution)/shard_map/scatter | solution.py:43
  98.5 2.2 fusion.7
  100.8 30.5 %while.33 = (s32[]{:T(128)}, f32[4,128,128]{2,1,0:T(8,128)S(1)}, s32[]{:T(128)}, f32[8,4,128,128]{3,2,1,0:T(8,128)}, s32[8]{0:T(128)S(1)}, /*index=5*/s32[8]{0:T(128)S(1)}, f32[8,4,128,128]{3,2,1,0:T(8,128)}) while((s32[]{:T(128)}, f32[4,128,128]{2,1,0:T(8,128)S(1)}, s32[]{:T(128)}, f32[8,4,128,128]{3,2,1,0:T(8,128)}, ...), condition=%wide.region_3.5_spmd.clone.clone, body=%wide.region_2.4_spmd.clone.sunk.clone | while | flops 327685 | bytes 1310871 | solution.py:73
  132.0 5.0 %all-to-all-start.2 = ((bf16[32,48,512]{2,1,0:T(8,128)(2,1)}), bf16[32,48,512]{2,1,0:T(8,128)(2,1)}, u32[]{:S(2)}, u32[]{:S(2)}) async-start(bf16[32,48,512]{2,1,0:T(8,128)(2,1)} %get-tuple-element.211), calls=%async_computation.2 | async-start | bytes 3145728 | tf_op jit(solution)/shard_map/all_to_all | solution.py:51
  137.8 25.2 %all-to-all-done.2 = bf16[32,48,512]{2,1,0:T(8,128)(2,1)} async-done(((bf16[32,48,512]{2,1,0:T(8,128)(2,1)}), bf16[32,48,512]{2,1,0:T(8,128)(2,1)}, u32[]{:S(2)}, u32[]{:S(2)}) %all-to-all-start.2) | async-done | bytes 1572896 | tf_op jit(solution)/shard_map/all_to_all | solution.py:51
  163.0 8.0 %scatter_custom_fusion.2 = bf16[1025,512]{1,0:T(8,128)(2,1)S(1)} fusion(s32[1536]{0:T(1024)S(1)} %fusion.23, bf16[1536,512]{1,0:T(8,128)(2,1)} %bitcast.8, bf16[]{:T(256)} %constant.68.clone.1), kind=kCustom, calls=%fused_computation.35 | custom fusion | bytes 1050112 | tf_op jit(solution)/shard_map/scatter | solution.py:43
  174.2 62.0 %all-reduce.4 = f32[32]{0:T(128)S(1)} all-reduce(f32[32]{0:T(128)S(1)} %dynamic-update-slice), channel_id=1, replica_groups=mesh['seq'=32,'head'=8] {'seq'}, use_global_device_ids=true, to_apply=%add.4 | all-reduce | flops 32 | bytes 256
  236.2 74.8 %while.34 = (s32[]{:T(128)}, f32[4,128,128]{2,1,0:T(8,128)S(1)}, s32[]{:T(128)}, f32[32,4,128,128]{3,2,1,0:T(8,128)}, f32[32]{0:T(128)S(1)}, /*index=5*/f32[1]{0:T(128)}) while((s32[]{:T(128)}, f32[4,128,128]{2,1,0:T(8,128)S(1)}, s32[]{:T(128)}, f32[32,4,128,128]{3,2,1,0:T(8,128)}, f32[32]{0:T(128)S(1)}, ...), condition=%wide.region_5.7_spmd.clone.clone, body=%wide.region_4.6_spmd.clone.sunk.clone | while | flops 262149 | bytes 786561 | solution.py:25
  310.9 3.9 fusion.2
  314.8 4.5 %multiply_reduce_fusion = (f32[8,128]{1,0:T(8,128)S(1)}, f32[8,128,4,128]{1,3,2,0:T(8,128)}) fusion(f32[8,4,128,128]{3,2,1,0:T(8,128)} %fusion.2, bf16[8,128,4,128]{1,3,2,0:T(8,128)(2,1)S(1)} %copy.28, pred[128,128]{1,0:T(8,128)(4,1)S(1)} %iota_compare_fusion, bf16[8,128,4,128]{3,2,1,0:T(4,128)(2,1)S(1)} %reshape.215, bf16[8,128,4,128]{3,2,1,0:T(4,128)(2,1)S(1)} %reshape.217), kind=kOutput, calls=%fused_computation.15 | convolution fusion | flops 271055872 | bytes 7360512 | tf_op jit(solution)/shard_map/chts,cshe->cthe/dot_general | solution.py:93
  319.4 16.5 %psum.7 = f32[1024]{0:T(1024)S(1)} all-reduce(f32[1024]{0:T(1024)S(1)} %bitcast.63), channel_id=1, replica_groups=mesh['seq'=32,'head'=8] {'head'}, use_global_device_ids=true, to_apply=%region_8.10 | all-reduce | flops 1024 | bytes 8192 | tf_op jit(solution)/shard_map/psum | solution.py:98
  338.2 5.4 %gather_fusion.3 = bf16[1536,512]{1,0:T(8,128)(2,1)} fusion(bf16[1025,512]{1,0:T(8,128)(2,1)S(1)} %concatenate.15, s32[2048]{0:T(1024)S(1)} %pad_clamp_fusion), kind=kCustom, calls=%fused_computation.3.clone | custom fusion | bytes 3151872 | tf_op jit(solution)/shard_map/jit(_take)/gather | solution.py:36
  343.6 2.8 broadcast_select_fusion
  346.4 11.1 %all-to-all-start.3 = ((bf16[32,48,512]{2,1,0:T(8,128)(2,1)}), bf16[32,48,512]{2,1,0:T(8,128)(2,1)S(1)}, u32[]{:S(2)}, u32[]{:S(2)}) async-start(bf16[32,48,512]{2,1,0:T(8,128)(2,1)} %broadcast_select_fusion), calls=%async_computation.3 | async-start | bytes 3145728 | tf_op jit(solution)/shard_map/all_to_all | solution.py:100
  357.7 22.6 %all-to-all-done.3 = bf16[32,48,512]{2,1,0:T(8,128)(2,1)S(1)} async-done(((bf16[32,48,512]{2,1,0:T(8,128)(2,1)}), bf16[32,48,512]{2,1,0:T(8,128)(2,1)S(1)}, u32[]{:S(2)}, u32[]{:S(2)}) %all-to-all-start.3) | async-done | bytes 1572896 | tf_op jit(solution)/shard_map/all_to_all | solution.py:100
  381.5 8.0 %scatter_custom_fusion.3 = bf16[1025,512]{1,0:T(8,128)(2,1)S(1)} fusion(s32[1536]{0:T(1024)S(1)} %fusion.22, bf16[1536,512]{1,0:T(8,128)(2,1)} %bitcast.61, bf16[]{:T(256)} %constant.68.clone.1), kind=kCustom, calls=%fused_computation.33 | custom fusion | bytes 1050112 | tf_op jit(solution)/shard_map/scatter | solution.py:43
  (149 shorter events, 89.8 us)
Async XLA Ops:
  8.1 1.5 copy-start.2
  15.1 5.4 %copy-start.3 = (bf16[1024,512]{1,0:T(8,128)(2,1)S(1)}, bf16[1024,512]{1,0:T(8,128)(2,1)}, u32[]{:S(2)}) copy-start(bf16[1024,512]{1,0:T(8,128)(2,1)} %param.14) | copy-start | bytes 3145732
  61.1 4.7 %copy-start.4 = (s32[32,48]{1,0:T(8,128)S(1)}, s32[32,48]{1,0:T(8,128)}, u32[]{:S(2)}) copy-start(s32[32,48]{1,0:T(8,128)} %param.16) | copy-start | bytes 18436
  61.1 27.0 %all-to-all-start = ((bf16[32,48,512]{2,1,0:T(8,128)(2,1)}), bf16[32,48,512]{2,1,0:T(8,128)(2,1)}, u32[]{:S(2)}, u32[]{:S(2)}) async-start(bf16[32,48,512]{2,1,0:T(8,128)(2,1)} %get-tuple-element.213), calls=%async_computation | async-start | bytes 3145728 | tf_op jit(solution)/shard_map/all_to_all | solution.py:54
  65.8 170.4 %all-gather.3.cloned.1.call-start = ((), (), s32[]{:S(2)}) async-start(), calls=%async_computation.4 | async-start | bytes 8650752 | tf_op jit(solution)/shard_map/all_gather | solution.py:16
  98.5 2.2 copy-start.6
  131.2 0.7 copy-start
  132.0 5.1 %copy-start.7 = (u32[256]{0:T(256)S(1)}, u32[256]{0:T(256)}, u32[]{:S(2)}) copy-start(u32[256]{0:T(256)} %constant.88) | copy-start | bytes 3076
  132.0 31.0 %all-to-all-start.2 = ((bf16[32,48,512]{2,1,0:T(8,128)(2,1)}), bf16[32,48,512]{2,1,0:T(8,128)(2,1)}, u32[]{:S(2)}, u32[]{:S(2)}) async-start(bf16[32,48,512]{2,1,0:T(8,128)(2,1)} %get-tuple-element.211), calls=%async_computation.2 | async-start | bytes 3145728 | tf_op jit(solution)/shard_map/all_to_all | solution.py:51
  346.4 11.2 %copy-start.5 = (s32[32,48]{1,0:T(8,128)S(1)}, s32[32,48]{1,0:T(8,128)}, u32[]{:S(2)}) copy-start(s32[32,48]{1,0:T(8,128)} %param.15) | copy-start | bytes 18436
  346.4 33.9 %all-to-all-start.3 = ((bf16[32,48,512]{2,1,0:T(8,128)(2,1)}), bf16[32,48,512]{2,1,0:T(8,128)(2,1)S(1)}, u32[]{:S(2)}, u32[]{:S(2)}) async-start(bf16[32,48,512]{2,1,0:T(8,128)(2,1)} %broadcast_select_fusion), calls=%async_computation.3 | async-start | bytes 3145728 | tf_op jit(solution)/shard_map/all_to_all | solution.py:100
  380.3 1.2 copy-start.1
Sparse Core Ops, SparseCore 0:
  132.1 65.4 all-gather.2
where the time goes:
time: 400 us; the launch traced here: 397 us
  blocking collectives  110 us (28%)
  local copies, waits for them, and re-layouts  91.7 us (23%)
  waiting for transfers between devices  61 us (15%)
  other arithmetic  58.3 us (15%)
  loops' own time  31.5 us (8%)
  starting transfers between devices  20.8 us (5%)
  between operations  13.7 us (3%)
  matrix products  10.7 us (3%)
    unnamed x1, blocking collectives  62 us
    select_n x31, other arithmetic, lap(): jnp.where(position < mine, new, old)  35.6 us
    scatter x4, local copies, waits for them, and re-layouts, place_rows(): placed = jnp.zeros((tok_count + 1, row_width), arrived.dtype).at[slot_tab...  31.9 us
    all_to_all x1, blocking collectives, shards(): lax.all_to_all(pack_rows(value_vectors, send_slots), 'seq', split_axis=0,...  31.3 us
    all_to_all x1, waiting for transfers between devices, shards(): lax.all_to_all(pack_rows(query_vectors, send_slots), 'seq', split_axis=0,...  25.2 us
    all_to_all x1, waiting for transfers between devices, shards(): lax.all_to_all(pack_rows(normed, receive_slots), 'seq', split_axis=0, con...  22.6 us
    gather x4, local copies, waits for them, and re-layouts, pack_rows(): return jnp.take(padded, slot_table, axis=0)  21.7 us
    another operation x1, loops' own time, prefix(): return lax.fori_loop(0, count - 1, lap, subtotal)  20.9 us
  transfers between devices with their start and end apart: 4, of which 3 were waited for; matrix products, arithmetic and copies ran while one was open for 5% of the time, Pallas kernels for 0%

commit v1 on v0

v1 whole, which is shorter than its diff:
```python
import functools

import jax
import jax.numpy as jnp
from jax import lax
from jax.experimental import pallas as pl
from jax.experimental.pallas import tpu as pltpu
from jax.sharding import PartitionSpec as P

H = 32
HD = 128
CH = 128
CAP = 48
N_SEQ = 32
N_HEAD = 8
TOK = 1024
WIDE = 512
COLS = 256
SLOTS = N_SEQ * CAP
GROUPS = TOK // CH
PIECE = COLS // N_SEQ
MESH = pl.DeviceIdType.MESH
BF16 = jnp.bfloat16
F32 = jnp.float32

epsilon = 1e-05

K0, V0, K1, V1, Q0, Q1, R0, R1 = range(8)


def kernel(
    q_ref, k_ref, v_ref, tab_ref, resets_ref, out_ref,
    pack_send, place_send, pack_recv, place_recv,
    outbox, inbox, q_ctx, k_ctx, v_ctx, raw, kv, carried, state_out, state_in, prefix_out, prefix_in,
    back, z_box,
    bulk_ssem, bulk_rsem, st_ssem, st_rsem, pf_ssem, pf_rsem, z_ssem, z_rsem,
):
    me = lax.axis_index("seq")
    mine = lax.axis_index("head")

    barrier = pltpu.get_barrier_semaphore()

    @pl.loop(1, N_SEQ)
    def _(k):
        pl.semaphore_signal(
            barrier, inc=1, device_id={"seq": lax.rem(me + k, N_SEQ), "head": mine}, device_id_type=MESH
        )

    @pl.loop(1, N_HEAD)
    def _(k):
        pl.semaphore_signal(
            barrier, inc=1, device_id={"seq": me, "head": lax.rem(mine + k, N_HEAD)}, device_id_type=MESH
        )

    diagonal = (
        lax.broadcasted_iota(jnp.int32, (128, 128), 0) == lax.broadcasted_iota(jnp.int32, (128, 128), 1)
    )

    def to_column(row):
        return jnp.sum(jnp.where(diagonal, jnp.broadcast_to(row, (128, 128)), 0.0), axis=1, keepdims=True)

    def to_row(column):
        return jnp.sum(jnp.where(diagonal, jnp.broadcast_to(column, (128, 128)), 0.0), axis=0, keepdims=True)

    def build_pack(table, pack):
        @pl.loop(0, SLOTS // 128)
        def _(i):
            column = to_column(tab_ref[pl.ds(table * 12 + i, 1), :].astype(F32))
            spots = lax.broadcasted_iota(jnp.int32, (128, TOK), 1).astype(F32)
            pack[pl.ds(pl.multiple_of(i * 128, 128), 128), :] = jnp.where(spots == column, 1.0, 0.0).astype(BF16)

    def build_place(table, place):
        for i in range(SLOTS // 128):
            row = tab_ref[table * 12 + i : table * 12 + i + 1, :]

            @pl.loop(0, TOK // 256)
            def _(j):
                spots = lax.broadcasted_iota(jnp.int32, (256, 128), 0) + j * 256
                place[pl.ds(pl.multiple_of(j * 256, 256), 256), i * 128 : (i + 1) * 128] = jnp.where(
                    spots == row, 1.0, 0.0
                ).astype(BF16)

    def pack_rows(pack, rows_ref, half, stage):
        @pl.loop(0, SLOTS // 384)
        def _(i):
            here = pl.ds(pl.multiple_of(i * 384, 384), 384)
            outbox[stage, here, :] = jnp.dot(
                pack[here, :], rows_ref[:, half * COLS : (half + 1) * COLS], preferred_element_type=F32
            ).astype(BF16)

    def place_rows(place, stage, rows_ref, half):
        @pl.loop(0, TOK // 256)
        def _(i):
            here = pl.ds(pl.multiple_of(i * 256, 256), 256)
            rows_ref[here, half * COLS : (half + 1) * COLS] = jnp.dot(
                place[here, :], inbox[stage], preferred_element_type=F32
            ).astype(BF16)

    def block(device):
        return pl.ds(pl.multiple_of(device * CAP, CAP), CAP)

    def send_bulk(stage):
        @pl.loop(1, N_SEQ)
        def _(k):
            peer = lax.rem(me + k, N_SEQ)
            pltpu.make_async_remote_copy(
                src_ref=outbox.at[stage, block(peer), :],
                dst_ref=inbox.at[stage, block(me), :],
                send_sem=bulk_ssem.at[stage],
                recv_sem=bulk_rsem.at[stage],
                device_id={"seq": peer, "head": mine},
                device_id_type=MESH,
            ).start()

        inbox[stage, block(me), :] = outbox[stage, block(me), :]

    def all_bulk(stage):
        most = pl.ds(0, SLOTS - CAP)
        return pltpu.make_async_remote_copy(
            src_ref=outbox.at[stage, most, :],
            dst_ref=inbox.at[stage, most, :],
            send_sem=bulk_ssem.at[stage],
            recv_sem=bulk_rsem.at[stage],
            device_id={"seq": me, "head": mine},
            device_id_type=MESH,
        )

    def send_small(source, target, half, ssem, rsem):
        @pl.loop(1, N_SEQ)
        def _(k):
            peer = lax.rem(me + k, N_SEQ)
            pltpu.make_async_remote_copy(
                src_ref=source.at[half, peer],
                dst_ref=target.at[half, me],
                send_sem=ssem.at[half],
                recv_sem=rsem.at[half],
                device_id={"seq": peer, "head": mine},
                device_id_type=MESH,
            ).start()

        target[half, me] = source[half, me]

    def all_small(source, target, half, ssem, rsem):
        return pltpu.make_async_remote_copy(
            src_ref=source.at[half, pl.ds(0, N_SEQ - 1)],
            dst_ref=target.at[half, pl.ds(0, N_SEQ - 1)],
            send_sem=ssem.at[half],
            recv_sem=rsem.at[half],
            device_id={"seq": me, "head": mine},
            device_id_type=MESH,
        )

    def keep_of(group):
        return 1.0 - resets_ref[group].astype(F32)

    def group_states(half):
        state = [jnp.zeros((HD, HD), F32), jnp.zeros((HD, HD), F32)]
        kept = jnp.float32(1.0)
        for c in range(GROUPS):
            keep = keep_of(c)
            kept = kept * keep
            for h in range(2):
                cols = slice(half * COLS + h * HD, half * COLS + (h + 1) * HD)
                rows = slice(c * CH, (c + 1) * CH)
                group_kv = lax.dot_general(
                    k_ctx[rows, cols], v_ctx[rows, cols], (((0,), (0,)), ((), ())), preferred_element_type=F32
                )
                kv[half, c, h * HD : (h + 1) * HD, :] = group_kv
                state[h] = state[h] * keep + group_kv
        for h in range(2):
            state_out[half, h * 16 : (h + 1) * 16, 0:PIECE, :] = state[h].reshape(16, PIECE, HD)
        state_out[half, :, PIECE : PIECE + 8, :] = jnp.broadcast_to(kept, (N_SEQ, 8, HD))

    def prefixes(half):
        total = jnp.zeros((PIECE, HD), F32)
        for s in range(N_SEQ):
            prefix_out[half, s] = total
            total = state_in[half, s, 0:PIECE, :] + state_in[half, s, PIECE : PIECE + 8, :] * total

    def attend(half):
        causal = (
            lax.broadcasted_iota(jnp.int32, (CH, CH), 0) >= lax.broadcasted_iota(jnp.int32, (CH, CH), 1)
        )
        for h in range(2):
            state = prefix_in[half, h * 16 : (h + 1) * 16].reshape(HD, HD)
            for c in range(GROUPS):
                state = state * keep_of(c)
                carried[half, c, h * HD : (h + 1) * HD, :] = state.astype(BF16)
                state = state + kv[half, c, h * HD : (h + 1) * HD, :]
        for c in range(GROUPS):
            for h in range(2):
                cols = slice(half * COLS + h * HD, half * COLS + (h + 1) * HD)
                rows = slice(c * CH, (c + 1) * CH)
                q = q_ctx[rows, cols]
                scores = lax.dot_general(
                    q, k_ctx[rows, cols], (((1,), (1,)), ((), ())), preferred_element_type=F32
                )
                weights = jnp.where(causal, scores, 0.0).astype(BF16)
                raw[rows, cols] = (
                    jnp.dot(q, carried[half, c, h * HD : (h + 1) * HD, :], preferred_element_type=F32)
                    + jnp.dot(weights, v_ctx[rows, cols], preferred_element_type=F32)
                ).astype(BF16)

    build_pack(0, pack_send)
    pack_rows(pack_send, k_ref, 0, K0)
    pl.semaphore_wait(barrier, N_SEQ - 1 + N_HEAD - 1)
    send_bulk(K0)
    pack_rows(pack_send, v_ref, 0, V0)
    send_bulk(V0)
    pack_rows(pack_send, k_ref, 1, K1)
    build_place(1, place_recv)
    pack_rows(pack_send, v_ref, 1, V1)
    all_bulk(K0).wait_send()
    send_bulk(K1)
    pack_rows(pack_send, q_ref, 0, Q0)
    pack_rows(pack_send, q_ref, 1, Q1)
    build_pack(1, pack_recv)
    build_place(0, place_send)
    all_bulk(K0).wait_recv()
    place_rows(place_recv, K0, k_ctx, 0)
    all_bulk(V0).wait_send()
    send_bulk(V1)
    all_bulk(V0).wait_recv()
    place_rows(place_recv, V0, v_ctx, 0)
    group_states(0)
    send_small(state_out, state_in, 0, st_ssem, st_rsem)
    all_bulk(K1).wait_send()
    send_bulk(Q0)
    all_small(state_out, state_in, 0, st_ssem, st_rsem).wait_recv()
    prefixes(0)
    send_small(prefix_out, prefix_in, 0, pf_ssem, pf_rsem)
    all_bulk(K1).wait_recv()
    place_rows(place_recv, K1, k_ctx, 1)
    all_bulk(V1).wait_send()
    send_bulk(Q1)
    all_bulk(V1).wait_recv()
    place_rows(place_recv, V1, v_ctx, 1)
    group_states(1)
    send_small(state_out, state_in, 1, st_ssem, st_rsem)
    all_small(state_out, state_in, 1, st_ssem, st_rsem).wait_recv()
    prefixes(1)
    send_small(prefix_out, prefix_in, 1, pf_ssem, pf_rsem)
    all_small(prefix_out, prefix_in, 0, pf_ssem, pf_rsem).wait_recv()
    all_bulk(Q0).wait_recv()
    place_rows(place_recv, Q0, q_ctx, 0)
    attend(0)
    pack_rows(pack_recv, raw, 0, R0)
    send_bulk(R0)
    all_small(prefix_out, prefix_in, 1, pf_ssem, pf_rsem).wait_recv()
    all_bulk(Q1).wait_recv()
    place_rows(place_recv, Q1, q_ctx, 1)
    attend(1)
    pack_rows(pack_recv, raw, 1, R1)
    send_bulk(R1)
    all_bulk(R0).wait_recv()
    place_rows(place_send, R0, back, 0)
    all_bulk(R1).wait_recv()
    place_rows(place_send, R1, back, 1)

    for c in range(TOK // 128):
        rows = back[c * 128 : (c + 1) * 128, :].astype(F32)
        z_box[mine, c : c + 1, :] = to_row(jnp.sum(rows * rows, axis=1, keepdims=True))

    @pl.loop(1, N_HEAD)
    def _(k):
        pltpu.make_async_remote_copy(
            src_ref=z_box.at[mine],
            dst_ref=z_box.at[mine],
            send_sem=z_ssem,
            recv_sem=z_rsem,
            device_id={"seq": me, "head": lax.rem(mine + k, N_HEAD)},
            device_id_type=MESH,
        ).start()

    all_z = pltpu.make_async_remote_copy(
        src_ref=z_box.at[pl.ds(0, N_HEAD - 1)],
        dst_ref=z_box.at[pl.ds(0, N_HEAD - 1)],
        send_sem=z_ssem,
        recv_sem=z_rsem,
        device_id={"seq": me, "head": mine},
        device_id_type=MESH,
    )
    all_z.wait_recv()
    squares = z_box[0]
    for z in range(1, N_HEAD):
        squares = squares + z_box[z]
    scale = lax.rsqrt(squares / (H * HD) + epsilon)
    for c in range(TOK // 128):
        rows = slice(c * 128, (c + 1) * 128)
        out_ref[rows, :] = (back[rows, :].astype(F32) * to_column(scale[c : c + 1, :])).astype(BF16)

    all_z.wait_send()
    for stage in (Q0, Q1, R0, R1):
        all_bulk(stage).wait_send()
    for half in range(2):
        all_small(state_out, state_in, half, st_ssem, st_rsem).wait_send()
        all_small(prefix_out, prefix_in, half, pf_ssem, pf_rsem).wait_send()


def shards(query_vectors, key_vectors, value_vectors, send_slots, receive_slots, resets):
    tables = jnp.concatenate([send_slots.reshape(SLOTS // 128, 128), receive_slots.reshape(SLOTS // 128, 128)], 0)
    vmem = pl.BlockSpec(memory_space=pltpu.VMEM)
    square = lambda rows, columns: pltpu.VMEM((rows, columns), BF16)
    return pl.pallas_call(
        kernel,
        name="attention",
        out_shape=jax.ShapeDtypeStruct((TOK, WIDE), BF16),
        in_specs=[vmem, vmem, vmem, vmem, pl.BlockSpec(memory_space=pltpu.SMEM)],
        out_specs=vmem,
        scratch_shapes=[
            square(SLOTS, TOK), square(TOK, SLOTS), square(SLOTS, TOK), square(TOK, SLOTS),
            pltpu.VMEM((8, SLOTS, COLS), BF16), pltpu.VMEM((8, SLOTS, COLS), BF16),
            square(TOK, WIDE), square(TOK, WIDE), square(TOK, WIDE), square(TOK, WIDE),
            pltpu.VMEM((2, GROUPS, COLS, HD), F32), pltpu.VMEM((2, GROUPS, COLS, HD), BF16),
            pltpu.VMEM((2, N_SEQ, PIECE + 8, HD), F32), pltpu.VMEM((2, N_SEQ, PIECE + 8, HD), F32),
            pltpu.VMEM((2, N_SEQ, PIECE, HD), F32), pltpu.VMEM((2, N_SEQ, PIECE, HD), F32),
            square(TOK, WIDE), pltpu.VMEM((N_HEAD, TOK // 128, 128), F32),
            pltpu.SemaphoreType.DMA((8,)), pltpu.SemaphoreType.DMA((8,)),
            pltpu.SemaphoreType.DMA((2,)), pltpu.SemaphoreType.DMA((2,)),
            pltpu.SemaphoreType.DMA((2,)), pltpu.SemaphoreType.DMA((2,)),
            pltpu.SemaphoreType.DMA, pltpu.SemaphoreType.DMA,
        ],
        compiler_params=pltpu.CompilerParams(
            collective_id=0, has_side_effects=True, vmem_limit_bytes=56 * 2**20
        ),
    )(query_vectors, key_vectors, value_vectors, tables, resets)


def solution(mesh):
    placed = (
        P("seq", "head"),
        P("seq", "head"),
        P("seq", "head"),
        P("seq", None),
        P("seq", None),
        P("seq"),
    )
    return jax.shard_map(shards, mesh=mesh, in_specs=placed, out_specs=P("seq", "head"), check_vma=False)
```

time: 400 us -> 121 us (0.30)
  Pallas kernels: 0 us -> 116 us
  blocking collectives: 110 us -> 0 us
  local copies, waits for them, and re-layouts: 91.7 us -> 3.14 us
  waiting for transfers between devices: 61 us -> 0 us
  other arithmetic: 58.3 us -> 0.61 us
  loops' own time: 31.5 us -> 0 us
  starting transfers between devices: 20.8 us -> 0 us
  between operations: 13.7 us -> 0.01 us
  matrix products: 10.7 us -> 0 us
    pallas_call x0 -> x1, Pallas kernels: none -> 116 us  [shards(): pl.pallas_call(kernel, name='attention', out_shape=jax.ShapeDtypeStruct((...]
    unnamed x1 -> x0, blocking collectives: 62 us -> none
    all_to_all x3 -> x0, waiting for transfers between devices: 61 us -> none  [the longest x1 25.2 us: shards(): lax.all_to_all(pack_rows(query_vectors, send_slots), 'seq', split_axis=0,...]
    select_n x37 -> x0, other arithmetic: 43 us -> none  [the longest x31 35.6 us: lap(): jnp.where(position < mine, new, old)]
    scatter x4 -> x0, local copies, waits for them, and re-layouts: 31.9 us -> none  [place_rows(): placed = jnp.zeros((tok_count + 1, row_width), arrived.dtype).at[slot_tab...]
    another operation x2 -> x0, loops' own time: 31.5 us -> none  [the longest x1 20.9 us: prefix(): return lax.fori_loop(0, count - 1, lap, subtotal)]
    all_to_all x1 -> x0, blocking collectives: 31.3 us -> none  [shards(): lax.all_to_all(pack_rows(value_vectors, send_slots), 'seq', split_axis=0,...]
    dynamic_slice x39 -> x0, local copies, waits for them, and re-layouts: 22.9 us -> none  [the longest x31 18.2 us: lap(): longer = join(subtotal, jax.tree.map(lambda part: part[position], pieces))]
  transfers between devices with their start and end apart: 4 -> 0, of which waited for: 3 -> 0; matrix products, arithmetic and copies ran while one was open for 5% -> 0% of each run, Pallas kernels for 0% -> 0%
where the time goes in v1:
time: 121 us; the launch traced here: 120 us
  Pallas kernels  116 us (96%)
  local copies, waits for them, and re-layouts  3.14 us (3%)
    pallas_call x1, Pallas kernels, shards(): pl.pallas_call(kernel, name='attention', out_shape=jax.ShapeDtypeStruct((...  116 us

profile of v1, /device:TPU:1, one launch (start us, length us, event | category | flops | bytes accessed | tf_op | source)
XLA Modules:
  0.0 119.8 jit_solution(8176616088958156938)
XLA Ops:
  0.0 0.0 copy-start
  0.0 0.8 reshape.6
  0.8 0.0 copy-done
  0.8 0.1 reshape.7
  0.9 0.6 pad_add_fusion.tab_ref
  1.5 116.0 %attention.1 = bf16[1024,512]{1,0:T(8,128)(2,1)} custom-call(bf16[1024,512]{1,0:T(8,128)(2,1)} %q_ref.1, bf16[1024,512]{1,0:T(8,128)(2,1)} %k_ref.1, bf16[1024,512]{1,0:T(8,128)(2,1)} %v_ref.1, s32[24,128]{1,0:T(8,128)} %pad_add_fusion.tab_ref, s32[8]{0:T(128)} %resets_ref.1), custom_call_target="tpu_custom_call" | custom-call | tf_op jit(solution)/shard_map/attention/pallas_call | solution.py:304
  117.5 2.3 %copy.8 = bf16[1024,512]{1,0:T(8,128)(2,1)} copy(bf16[1024,512]{1,0:T(8,128)(2,1)} %attention.1) | data formatting | bytes 2097152
Async XLA Ops:
  0.0 0.8 copy-start

commit v2 on v1

--- a/solution.py
+++ b/solution.py
@@ -29,10 +29,11 @@
 
 
 def kernel(
-    q_ref, k_ref, v_ref, tab_ref, resets_ref, out_ref,
+    q_hbm, k_hbm, v_hbm, send_ref, receive_ref, resets_ref, back, scale_ref,
+    q_ref, k_ref, v_ref, columns,
     pack_send, place_send, pack_recv, place_recv,
     outbox, inbox, q_ctx, k_ctx, v_ctx, raw, kv, carried, state_out, state_in, prefix_out, prefix_in,
-    back, z_box,
+    z_box, in_sem,
     bulk_ssem, bulk_rsem, st_ssem, st_rsem, pf_ssem, pf_rsem, z_ssem, z_rsem,
 ):
     me = lax.axis_index("seq")
@@ -52,6 +53,13 @@
             barrier, inc=1, device_id={"seq": me, "head": lax.rem(mine + k, N_HEAD)}, device_id_type=MESH
         )
 
+    staged = [
+        pltpu.make_async_copy(source, target, in_sem.at[i])
+        for i, (source, target) in enumerate([(k_hbm, k_ref), (v_hbm, v_ref), (q_hbm, q_ref)])
+    ]
+    for copy in staged:
+        copy.start()
+
     diagonal = (
         lax.broadcasted_iota(jnp.int32, (128, 128), 0) == lax.broadcasted_iota(jnp.int32, (128, 128), 1)
     )
@@ -62,20 +70,22 @@
     def to_row(column):
         return jnp.sum(jnp.where(diagonal, jnp.broadcast_to(column, (128, 128)), 0.0), axis=0, keepdims=True)
 
-    def build_pack(table, pack):
-        @pl.loop(0, SLOTS // 128)
-        def _(i):
-            column = to_column(tab_ref[pl.ds(table * 12 + i, 1), :].astype(F32))
-            spots = lax.broadcasted_iota(jnp.int32, (128, TOK), 1).astype(F32)
-            pack[pl.ds(pl.multiple_of(i * 128, 128), 128), :] = jnp.where(spots == column, 1.0, 0.0).astype(BF16)
-
-    def build_place(table, place):
+    def build_pack(table_ref, pack):
+        corner = diagonal[:CAP, :CAP]
+        for d in range(N_SEQ):
+            row = jnp.broadcast_to(table_ref[d : d + 1, :].astype(F32), (CAP, CAP))
+            column = jnp.sum(jnp.where(corner, row, 0.0), axis=1, keepdims=True)
+            spots = lax.broadcasted_iota(jnp.int32, (CAP, TOK), 1).astype(F32)
+            pack[d * CAP : (d + 1) * CAP, :] = jnp.where(spots == column, 1.0, 0.0).astype(BF16)
+            columns[d * CAP : (d + 1) * CAP, :] = column
+
+    def build_place(place):
         for i in range(SLOTS // 128):
-            row = tab_ref[table * 12 + i : table * 12 + i + 1, :]
+            row = to_row(columns[i * 128 : (i + 1) * 128, :])
 
             @pl.loop(0, TOK // 256)
             def _(j):
-                spots = lax.broadcasted_iota(jnp.int32, (256, 128), 0) + j * 256
+                spots = (lax.broadcasted_iota(jnp.int32, (256, 128), 0) + j * 256).astype(F32)
                 place[pl.ds(pl.multiple_of(j * 256, 256), 256), i * 128 : (i + 1) * 128] = jnp.where(
                     spots == row, 1.0, 0.0
                 ).astype(BF16)
@@ -102,7 +112,7 @@
     def send_bulk(stage):
         @pl.loop(1, N_SEQ)
         def _(k):
-            peer = lax.rem(me + k, N_SEQ)
+            peer = lax.rem(me + 13 * k, N_SEQ)
             pltpu.make_async_remote_copy(
                 src_ref=outbox.at[stage, block(peer), :],
                 dst_ref=inbox.at[stage, block(me), :],
@@ -128,7 +138,7 @@
     def send_small(source, target, half, ssem, rsem):
         @pl.loop(1, N_SEQ)
         def _(k):
-            peer = lax.rem(me + k, N_SEQ)
+            peer = lax.rem(me + 13 * k, N_SEQ)
             pltpu.make_async_remote_copy(
                 src_ref=source.at[half, peer],
                 dst_ref=target.at[half, me],
@@ -201,21 +211,24 @@
                     + jnp.dot(weights, v_ctx[rows, cols], preferred_element_type=F32)
                 ).astype(BF16)
 
-    build_pack(0, pack_send)
+    build_pack(send_ref, pack_send)
+    staged[0].wait()
     pack_rows(pack_send, k_ref, 0, K0)
+    staged[1].wait()
+    pack_rows(pack_send, v_ref, 0, V0)
     pl.semaphore_wait(barrier, N_SEQ - 1 + N_HEAD - 1)
     send_bulk(K0)
-    pack_rows(pack_send, v_ref, 0, V0)
     send_bulk(V0)
+    build_place(place_send)
     pack_rows(pack_send, k_ref, 1, K1)
-    build_place(1, place_recv)
     pack_rows(pack_send, v_ref, 1, V1)
     all_bulk(K0).wait_send()
     send_bulk(K1)
+    staged[2].wait()
     pack_rows(pack_send, q_ref, 0, Q0)
     pack_rows(pack_send, q_ref, 1, Q1)
-    build_pack(1, pack_recv)
-    build_place(0, place_send)
+    build_pack(receive_ref, pack_recv)
+    build_place(place_recv)
     all_bulk(K0).wait_recv()
     place_rows(place_recv, K0, k_ctx, 0)
     all_bulk(V0).wait_send()
@@ -284,10 +297,7 @@
     squares = z_box[0]
     for z in range(1, N_HEAD):
         squares = squares + z_box[z]
-    scale = lax.rsqrt(squares / (H * HD) + epsilon)
-    for c in range(TOK // 128):
-        rows = slice(c * 128, (c + 1) * 128)
-        out_ref[rows, :] = (back[rows, :].astype(F32) * to_column(scale[c : c + 1, :])).astype(BF16)
+    scale_ref[...] = lax.rsqrt(squares / (H * HD) + epsilon)
 
     all_z.wait_send()
     for stage in (Q0, Q1, R0, R1):
@@ -297,33 +307,55 @@
         all_small(prefix_out, prefix_in, half, pf_ssem, pf_rsem).wait_send()
 
 
+def scale_rows(back_ref, scale_ref, out_ref):
+    diagonal = (
+        lax.broadcasted_iota(jnp.int32, (128, 128), 0) == lax.broadcasted_iota(jnp.int32, (128, 128), 1)
+    )
+    for c in range(TOK // 128):
+        rows = slice(c * 128, (c + 1) * 128)
+        spread = jnp.broadcast_to(scale_ref[c : c + 1, :], (128, 128))
+        column = jnp.sum(jnp.where(diagonal, spread, 0.0), axis=1, keepdims=True)
+        out_ref[rows, :] = (back_ref[rows, :].astype(F32) * column).astype(BF16)
+
+
 def shards(query_vectors, key_vectors, value_vectors, send_slots, receive_slots, resets):
-    tables = jnp.concatenate([send_slots.reshape(SLOTS // 128, 128), receive_slots.reshape(SLOTS // 128, 128)], 0)
     vmem = pl.BlockSpec(memory_space=pltpu.VMEM)
+    hbm = pl.BlockSpec(memory_space=pl.ANY)
     square = lambda rows, columns: pltpu.VMEM((rows, columns), BF16)
-    return pl.pallas_call(
+    back, scale = pl.pallas_call(
         kernel,
         name="attention",
-        out_shape=jax.ShapeDtypeStruct((TOK, WIDE), BF16),
-        in_specs=[vmem, vmem, vmem, vmem, pl.BlockSpec(memory_space=pltpu.SMEM)],
-        out_specs=vmem,
+        out_shape=[
+            jax.ShapeDtypeStruct((TOK, WIDE), BF16),
+            jax.ShapeDtypeStruct((TOK // 128, 128), F32),
+        ],
+        in_specs=[hbm, hbm, hbm, vmem, vmem, pl.BlockSpec(memory_space=pltpu.SMEM)],
+        out_specs=[vmem, vmem],
         scratch_shapes=[
+            square(TOK, WIDE), square(TOK, WIDE), square(TOK, WIDE), pltpu.VMEM((SLOTS, 1), F32),
             square(SLOTS, TOK), square(TOK, SLOTS), square(SLOTS, TOK), square(TOK, SLOTS),
             pltpu.VMEM((8, SLOTS, COLS), BF16), pltpu.VMEM((8, SLOTS, COLS), BF16),
             square(TOK, WIDE), square(TOK, WIDE), square(TOK, WIDE), square(TOK, WIDE),
             pltpu.VMEM((2, GROUPS, COLS, HD), F32), pltpu.VMEM((2, GROUPS, COLS, HD), BF16),
             pltpu.VMEM((2, N_SEQ, PIECE + 8, HD), F32), pltpu.VMEM((2, N_SEQ, PIECE + 8, HD), F32),
             pltpu.VMEM((2, N_SEQ, PIECE, HD), F32), pltpu.VMEM((2, N_SEQ, PIECE, HD), F32),
-            square(TOK, WIDE), pltpu.VMEM((N_HEAD, TOK // 128, 128), F32),
+            pltpu.VMEM((N_HEAD, TOK // 128, 128), F32), pltpu.SemaphoreType.DMA((3,)),
             pltpu.SemaphoreType.DMA((8,)), pltpu.SemaphoreType.DMA((8,)),
             pltpu.SemaphoreType.DMA((2,)), pltpu.SemaphoreType.DMA((2,)),
             pltpu.SemaphoreType.DMA((2,)), pltpu.SemaphoreType.DMA((2,)),
             pltpu.SemaphoreType.DMA, pltpu.SemaphoreType.DMA,
         ],
         compiler_params=pltpu.CompilerParams(
-            collective_id=0, has_side_effects=True, vmem_limit_bytes=56 * 2**20
+            collective_id=0, has_side_effects=True, vmem_limit_bytes=60 * 2**20
         ),
-    )(query_vectors, key_vectors, value_vectors, tables, resets)
+    )(query_vectors, key_vectors, value_vectors, send_slots, receive_slots, resets)
+    return pl.pallas_call(
+        scale_rows,
+        name="scale",
+        out_shape=jax.ShapeDtypeStruct((TOK, WIDE), BF16),
+        in_specs=[vmem, vmem],
+        out_specs=vmem,
+    )(back, scale)
 
 
 def solution(mesh):

time: 121 us -> 107 us (0.88)
  Pallas kernels: 116 us -> 107 us
  local copies, waits for them, and re-layouts: 3.14 us -> 0 us
    pallas_call x1 -> x2, Pallas kernels: 116 us -> 107 us  [the longest x1 104 us: shards(): pl.pallas_call(kernel, name='attention', out_shape=[jax.ShapeDtypeStruct(...]
    unnamed x3 -> x0, local copies, waits for them, and re-layouts: 2.27 us -> none
where the time goes in v2:
time: 107 us
  Pallas kernels  107 us (100%)
    pallas_call x1, Pallas kernels, shards(): pl.pallas_call(kernel, name='attention', out_shape=[jax.ShapeDtypeStruct(...  104 us
    pallas_call x1, Pallas kernels, shards(): pl.pallas_call(scale_rows, name='scale', out_shape=jax.ShapeDtypeStruct((...  2.47 us

profile of v2, /device:TPU:1, one launch (start us, length us, event | category | flops | bytes accessed | tf_op | source)
XLA Modules:
  0.0 106.9 jit_solution(15061203511847634004)
XLA Ops:
  0.0 104.4 %attention.1 = (bf16[1024,512]{1,0:T(8,128)(2,1)}, f32[8,128]{1,0:T(8,128)}) custom-call(bf16[1024,512]{1,0:T(8,128)(2,1)} %q_hbm.1, bf16[1024,512]{1,0:T(8,128)(2,1)} %k_hbm.1, bf16[1024,512]{1,0:T(8,128)(2,1)} %v_hbm.1, s32[32,48]{1,0:T(8,128)} %send_ref.1, s32[32,48]{1,0:T(8,128)} %receive_ref.1, s32[8]{0:T(128)} %resets_ref.1), custom_call_target="tpu_custom_call" | custom-call | tf_op jit(solution)/shard_map/attention/pallas_call | solution.py:325
  104.4 2.5 %scale.1 = bf16[1024,512]{1,0:T(8,128)(2,1)} custom-call(bf16[1024,512]{1,0:T(8,128)(2,1)} %get-tuple-element.7.back_ref, f32[8,128]{1,0:T(8,128)} %get-tuple-element.8.scale_ref), custom_call_target="tpu_custom_call" | custom-call | tf_op jit(solution)/shard_map/scale/pallas_call | solution.py:352

commit v3 on v2

--- a/solution.py
+++ b/solution.py
@@ -19,6 +19,7 @@
 SLOTS = N_SEQ * CAP
 GROUPS = TOK // CH
 PIECE = COLS // N_SEQ
+EARLY = 16
 MESH = pl.DeviceIdType.MESH
 BF16 = jnp.bfloat16
 F32 = jnp.float32
@@ -29,12 +30,12 @@
 
 
 def kernel(
-    q_hbm, k_hbm, v_hbm, send_ref, receive_ref, resets_ref, back, scale_ref,
+    q_hbm, k_hbm, v_hbm, send_ref, receive_ref, resets_ref, out_ref,
     q_ref, k_ref, v_ref, columns,
     pack_send, place_send, pack_recv, place_recv,
-    outbox, inbox, q_ctx, k_ctx, v_ctx, raw, kv, carried, state_out, state_in, prefix_out, prefix_in,
-    z_box, in_sem,
-    bulk_ssem, bulk_rsem, st_ssem, st_rsem, pf_ssem, pf_rsem, z_ssem, z_rsem,
+    outbox, inbox, q_ctx, k_ctx, v_ctx, raw, late_raw, kv, carried,
+    state_out, state_in, prefix_out, prefix_in, keeps, scale_out, scale_in, scale_parts, partial, z_box,
+    in_sem, bulk_ssem, bulk_rsem, st_ssem, st_rsem, pf_ssem, pf_rsem, row_ssem, row_rsem, z_ssem, z_rsem,
 ):
     me = lax.axis_index("seq")
     mine = lax.axis_index("head")
@@ -109,31 +110,46 @@
     def block(device):
         return pl.ds(pl.multiple_of(device * CAP, CAP), CAP)
 
-    def send_bulk(stage):
-        @pl.loop(1, N_SEQ)
-        def _(k):
-            peer = lax.rem(me + 13 * k, N_SEQ)
-            pltpu.make_async_remote_copy(
-                src_ref=outbox.at[stage, block(peer), :],
-                dst_ref=inbox.at[stage, block(me), :],
-                send_sem=bulk_ssem.at[stage],
-                recv_sem=bulk_rsem.at[stage],
-                device_id={"seq": peer, "head": mine},
-                device_id_type=MESH,
-            ).start()
-
-        inbox[stage, block(me), :] = outbox[stage, block(me), :]
-
-    def all_bulk(stage):
-        most = pl.ds(0, SLOTS - CAP)
+    def send_bulk(stage, parts=(0, 1)):
+        def send(part):
+            def one(k):
+                peer = lax.rem(me + 13 * k, N_SEQ)
+                pltpu.make_async_remote_copy(
+                    src_ref=outbox.at[stage, block(peer), :],
+                    dst_ref=inbox.at[stage, block(me), :],
+                    send_sem=bulk_ssem.at[stage, part],
+                    recv_sem=bulk_rsem.at[stage],
+                    device_id={"seq": peer, "head": mine},
+                    device_id_type=MESH,
+                ).start()
+
+            return one
+
+        if 0 in parts:
+            pl.loop(1, EARLY + 1)(send(0))
+            inbox[stage, block(me), :] = outbox[stage, block(me), :]
+        if 1 in parts:
+            pl.loop(EARLY + 1, N_SEQ)(send(1))
+
+    def bulk_of(stage, blocks, part):
+        rows = pl.ds(0, blocks * CAP)
         return pltpu.make_async_remote_copy(
-            src_ref=outbox.at[stage, most, :],
-            dst_ref=inbox.at[stage, most, :],
-            send_sem=bulk_ssem.at[stage],
+            src_ref=outbox.at[stage, rows, :],
+            dst_ref=inbox.at[stage, rows, :],
+            send_sem=bulk_ssem.at[stage, part],
             recv_sem=bulk_rsem.at[stage],
             device_id={"seq": me, "head": mine},
             device_id_type=MESH,
         )
+
+    def arrived(stage):
+        bulk_of(stage, N_SEQ - 1, 0).wait_recv()
+
+    def sent_early(stage):
+        bulk_of(stage, EARLY, 0).wait_send()
+
+    def sent_late(stage):
+        bulk_of(stage, N_SEQ - 1 - EARLY, 1).wait_send()
 
     def send_small(source, target, half, ssem, rsem):
         @pl.loop(1, N_SEQ)
@@ -160,15 +176,37 @@
             device_id_type=MESH,
         )
 
+    def send_rows(source_of, target, which):
+        @pl.loop(1, N_SEQ)
+        def _(k):
+            peer = lax.rem(me + 13 * k, N_SEQ)
+            pltpu.make_async_remote_copy(
+                src_ref=source_of(peer),
+                dst_ref=target.at[me],
+                send_sem=row_ssem.at[which],
+                recv_sem=row_rsem.at[which],
+                device_id={"seq": peer, "head": mine},
+                device_id_type=MESH,
+            ).start()
+
+    def all_rows(target, which):
+        most = pl.ds(0, N_SEQ - 1)
+        return pltpu.make_async_remote_copy(
+            src_ref=target.at[most],
+            dst_ref=target.at[most],
+            send_sem=row_ssem.at[which],
+            recv_sem=row_rsem.at[which],
+            device_id={"seq": me, "head": mine},
+            device_id_type=MESH,
+        )
+
     def keep_of(group):
         return 1.0 - resets_ref[group].astype(F32)
 
     def group_states(half):
         state = [jnp.zeros((HD, HD), F32), jnp.zeros((HD, HD), F32)]
-        kept = jnp.float32(1.0)
         for c in range(GROUPS):
             keep = keep_of(c)
-            kept = kept * keep
             for h in range(2):
                 cols = slice(half * COLS + h * HD, half * COLS + (h + 1) * HD)
                 rows = slice(c * CH, (c + 1) * CH)
@@ -178,14 +216,13 @@
                 kv[half, c, h * HD : (h + 1) * HD, :] = group_kv
                 state[h] = state[h] * keep + group_kv
         for h in range(2):
-            state_out[half, h * 16 : (h + 1) * 16, 0:PIECE, :] = state[h].reshape(16, PIECE, HD)
-        state_out[half, :, PIECE : PIECE + 8, :] = jnp.broadcast_to(kept, (N_SEQ, 8, HD))
+            state_out[half, h * 16 : (h + 1) * 16] = state[h].reshape(16, PIECE, HD)
 
     def prefixes(half):
         total = jnp.zeros((PIECE, HD), F32)
         for s in range(N_SEQ):
             prefix_out[half, s] = total
-            total = state_in[half, s, 0:PIECE, :] + state_in[half, s, PIECE : PIECE + 8, :] * total
+            total = state_in[half, s] + keeps[s] * total
 
     def attend(half):
         causal = (
@@ -198,81 +235,123 @@
                 carried[half, c, h * HD : (h + 1) * HD, :] = state.astype(BF16)
                 state = state + kv[half, c, h * HD : (h + 1) * HD, :]
         for c in range(GROUPS):
+            rows = slice(c * CH, (c + 1) * CH)
+            squares = jnp.zeros((CH, HD), F32)
             for h in range(2):
                 cols = slice(half * COLS + h * HD, half * COLS + (h + 1) * HD)
-                rows = slice(c * CH, (c + 1) * CH)
                 q = q_ctx[rows, cols]
                 scores = lax.dot_general(
                     q, k_ctx[rows, cols], (((1,), (1,)), ((), ())), preferred_element_type=F32
                 )
                 weights = jnp.where(causal, scores, 0.0).astype(BF16)
-                raw[rows, cols] = (
-                    jnp.dot(q, carried[half, c, h * HD : (h + 1) * HD, :], preferred_element_type=F32)
-                    + jnp.dot(weights, v_ctx[rows, cols], preferred_element_type=F32)
-                ).astype(BF16)
-
+                value = jnp.dot(q, carried[half, c, h * HD : (h + 1) * HD, :], preferred_element_type=F32)
+                value = value + jnp.dot(weights, v_ctx[rows, cols], preferred_element_type=F32)
+                squares = squares + value * value
+                if half == 0:
+                    raw[rows, cols] = value.astype(BF16)
+                else:
+                    late_raw[rows, h * HD : (h + 1) * HD] = value
+            row = to_row(jnp.sum(squares, axis=1, keepdims=True))
+            if half == 0:
+                partial[c : c + 1, :] = row
+            else:
+                z_box[mine, c : c + 1, :] = partial[c : c + 1, :] + row
+
+    slots = (
+        lax.broadcasted_iota(jnp.int32, (CAP, 128), 0) == lax.broadcasted_iota(jnp.int32, (CAP, 128), 1)
+    )
+
+    def normalize(scale):
+        lane = lax.broadcasted_iota(jnp.int32, (128, 128), 1)
+        for c in range(TOK // 128):
+            rows = slice(c * 128, (c + 1) * 128)
+            column = to_column(scale[c : c + 1, :])
+            raw[rows, COLS:] = (late_raw[rows, :] * column).astype(BF16)
+            rest = jnp.broadcast_to(column, (128, 128))
+            parts = jnp.zeros((128, 128), F32)
+            for i in range(3):
+                term = rest.astype(BF16).astype(F32)
+                parts = jnp.where(lane == i, term, parts)
+                rest = rest - term
+            scale_parts[rows, :] = parts.astype(BF16)
+
+    def pack_scales():
+        @pl.loop(0, SLOTS // 384)
+        def _(i):
+            here = pl.ds(pl.multiple_of(i * 384, 384), 384)
+            parts = jnp.dot(pack_recv[here, :], scale_parts[...], preferred_element_type=F32)
+            columns[here, :] = jnp.sum(parts, axis=1, keepdims=True)
+
+        for d in range(N_SEQ):
+            spread = jnp.broadcast_to(columns[d * CAP : (d + 1) * CAP, :], (CAP, 128))
+            scale_out[d] = jnp.sum(jnp.where(slots, spread, 0.0), axis=0, keepdims=True)
+        scale_in[me] = scale_out[me]
+
+    def scale_arrived():
+        for s in range(N_SEQ):
+            rows = slice(s * CAP, (s + 1) * CAP)
+            spread = jnp.broadcast_to(scale_in[s], (CAP, 128))
+            column = jnp.sum(jnp.where(slots, spread, 0.0), axis=1, keepdims=True)
+            inbox[R0, rows, :] = (inbox[R0, rows, :].astype(F32) * column).astype(BF16)
+
+    keep_all = jnp.float32(1.0)
+    for c in range(GROUPS):
+        keep_all = keep_all * keep_of(c)
+    keeps[me] = jnp.broadcast_to(keep_all, (1, 128))
     build_pack(send_ref, pack_send)
     staged[0].wait()
     pack_rows(pack_send, k_ref, 0, K0)
     staged[1].wait()
     pack_rows(pack_send, v_ref, 0, V0)
     pl.semaphore_wait(barrier, N_SEQ - 1 + N_HEAD - 1)
+    send_rows(lambda peer: keeps.at[me], keeps, 0)
     send_bulk(K0)
     send_bulk(V0)
     build_place(place_send)
     pack_rows(pack_send, k_ref, 1, K1)
     pack_rows(pack_send, v_ref, 1, V1)
-    all_bulk(K0).wait_send()
+    sent_late(K0)
     send_bulk(K1)
     staged[2].wait()
     pack_rows(pack_send, q_ref, 0, Q0)
     pack_rows(pack_send, q_ref, 1, Q1)
     build_pack(receive_ref, pack_recv)
     build_place(place_recv)
-    all_bulk(K0).wait_recv()
+    arrived(K0)
     place_rows(place_recv, K0, k_ctx, 0)
-    all_bulk(V0).wait_send()
-    send_bulk(V1)
-    all_bulk(V0).wait_recv()
+    arrived(V0)
     place_rows(place_recv, V0, v_ctx, 0)
     group_states(0)
     send_small(state_out, state_in, 0, st_ssem, st_rsem)
-    all_bulk(K1).wait_send()
-    send_bulk(Q0)
+    sent_early(K1)
+    send_bulk(V1)
+    arrived(K1)
+    place_rows(place_recv, K1, k_ctx, 1)
     all_small(state_out, state_in, 0, st_ssem, st_rsem).wait_recv()
+    all_rows(keeps, 0).wait_recv()
     prefixes(0)
     send_small(prefix_out, prefix_in, 0, pf_ssem, pf_rsem)
-    all_bulk(K1).wait_recv()
-    place_rows(place_recv, K1, k_ctx, 1)
-    all_bulk(V1).wait_send()
-    send_bulk(Q1)
-    all_bulk(V1).wait_recv()
+    sent_early(V1)
+    send_bulk(Q0)
+    arrived(V1)
     place_rows(place_recv, V1, v_ctx, 1)
     group_states(1)
     send_small(state_out, state_in, 1, st_ssem, st_rsem)
+    sent_early(Q0)
+    send_bulk(Q1)
+    all_small(prefix_out, prefix_in, 0, pf_ssem, pf_rsem).wait_recv()
+    arrived(Q0)
+    place_rows(place_recv, Q0, q_ctx, 0)
+    attend(0)
     all_small(state_out, state_in, 1, st_ssem, st_rsem).wait_recv()
     prefixes(1)
     send_small(prefix_out, prefix_in, 1, pf_ssem, pf_rsem)
-    all_small(prefix_out, prefix_in, 0, pf_ssem, pf_rsem).wait_recv()
-    all_bulk(Q0).wait_recv()
-    place_rows(place_recv, Q0, q_ctx, 0)
-    attend(0)
     pack_rows(pack_recv, raw, 0, R0)
-    send_bulk(R0)
+    send_bulk(R0, (0,))
+    arrived(Q1)
+    place_rows(place_recv, Q1, q_ctx, 1)
     all_small(prefix_out, prefix_in, 1, pf_ssem, pf_rsem).wait_recv()
-    all_bulk(Q1).wait_recv()
-    place_rows(place_recv, Q1, q_ctx, 1)
     attend(1)
-    pack_rows(pack_recv, raw, 1, R1)
-    send_bulk(R1)
-    all_bulk(R0).wait_recv()
-    place_rows(place_send, R0, back, 0)
-    all_bulk(R1).wait_recv()
-    place_rows(place_send, R1, back, 1)
-
-    for c in range(TOK // 128):
-        rows = back[c * 128 : (c + 1) * 128, :].astype(F32)
-        z_box[mine, c : c + 1, :] = to_row(jnp.sum(rows * rows, axis=1, keepdims=True))
 
     @pl.loop(1, N_HEAD)
     def _(k):
@@ -293,54 +372,60 @@
         device_id={"seq": me, "head": mine},
         device_id_type=MESH,
     )
+    send_bulk(R0, (1,))
     all_z.wait_recv()
     squares = z_box[0]
     for z in range(1, N_HEAD):
         squares = squares + z_box[z]
-    scale_ref[...] = lax.rsqrt(squares / (H * HD) + epsilon)
+    normalize(lax.rsqrt(squares / (H * HD) + epsilon))
+    pack_scales()
+    send_rows(lambda peer: scale_out.at[peer], scale_in, 1)
+    pack_rows(pack_recv, raw, 1, R1)
+    send_bulk(R1)
+    arrived(R0)
+    all_rows(scale_in, 1).wait_recv()
+    scale_arrived()
+    place_rows(place_send, R0, out_ref, 0)
+    arrived(R1)
+    place_rows(place_send, R1, out_ref, 1)
 
     all_z.wait_send()
-    for stage in (Q0, Q1, R0, R1):
-        all_bulk(stage).wait_send()
+    for stage in (K0, V0, Q1, R0, R1):
+        sent_early(stage)
+    for stage in (V0, K1, V1, Q0, Q1, R0, R1):
+        sent_late(stage)
     for half in range(2):
         all_small(state_out, state_in, half, st_ssem, st_rsem).wait_send()
         all_small(prefix_out, prefix_in, half, pf_ssem, pf_rsem).wait_send()
-
-
-def scale_rows(back_ref, scale_ref, out_ref):
-    diagonal = (
-        lax.broadcasted_iota(jnp.int32, (128, 128), 0) == lax.broadcasted_iota(jnp.int32, (128, 128), 1)
-    )
-    for c in range(TOK // 128):
-        rows = slice(c * 128, (c + 1) * 128)
-        spread = jnp.broadcast_to(scale_ref[c : c + 1, :], (128, 128))
-        column = jnp.sum(jnp.where(diagonal, spread, 0.0), axis=1, keepdims=True)
-        out_ref[rows, :] = (back_ref[rows, :].astype(F32) * column).astype(BF16)
+    all_rows(keeps, 0).wait_send()
+    all_rows(scale_in, 1).wait_send()
 
 
 def shards(query_vectors, key_vectors, value_vectors, send_slots, receive_slots, resets):
     vmem = pl.BlockSpec(memory_space=pltpu.VMEM)
     hbm = pl.BlockSpec(memory_space=pl.ANY)
     square = lambda rows, columns: pltpu.VMEM((rows, columns), BF16)
-    back, scale = pl.pallas_call(
+    row_of_each = lambda: pltpu.VMEM((N_SEQ, 1, 128), F32)
+    return pl.pallas_call(
         kernel,
         name="attention",
-        out_shape=[
-            jax.ShapeDtypeStruct((TOK, WIDE), BF16),
-            jax.ShapeDtypeStruct((TOK // 128, 128), F32),
-        ],
+        out_shape=pltpu.VMEM((TOK, WIDE), BF16),
         in_specs=[hbm, hbm, hbm, vmem, vmem, pl.BlockSpec(memory_space=pltpu.SMEM)],
-        out_specs=[vmem, vmem],
+        out_specs=vmem,
         scratch_shapes=[
             square(TOK, WIDE), square(TOK, WIDE), square(TOK, WIDE), pltpu.VMEM((SLOTS, 1), F32),
             square(SLOTS, TOK), square(TOK, SLOTS), square(SLOTS, TOK), square(TOK, SLOTS),
             pltpu.VMEM((8, SLOTS, COLS), BF16), pltpu.VMEM((8, SLOTS, COLS), BF16),
             square(TOK, WIDE), square(TOK, WIDE), square(TOK, WIDE), square(TOK, WIDE),
+            pltpu.VMEM((TOK, COLS), F32),
             pltpu.VMEM((2, GROUPS, COLS, HD), F32), pltpu.VMEM((2, GROUPS, COLS, HD), BF16),
-            pltpu.VMEM((2, N_SEQ, PIECE + 8, HD), F32), pltpu.VMEM((2, N_SEQ, PIECE + 8, HD), F32),
             pltpu.VMEM((2, N_SEQ, PIECE, HD), F32), pltpu.VMEM((2, N_SEQ, PIECE, HD), F32),
-            pltpu.VMEM((N_HEAD, TOK // 128, 128), F32), pltpu.SemaphoreType.DMA((3,)),
-            pltpu.SemaphoreType.DMA((8,)), pltpu.SemaphoreType.DMA((8,)),
+            pltpu.VMEM((2, N_SEQ, PIECE, HD), F32), pltpu.VMEM((2, N_SEQ, PIECE, HD), F32),
+            row_of_each(), row_of_each(), row_of_each(),
+            square(TOK, 128), pltpu.VMEM((TOK // 128, 128), F32), pltpu.VMEM((N_HEAD, TOK // 128, 128), F32),
+            pltpu.SemaphoreType.DMA((3,)),
+            pltpu.SemaphoreType.DMA((8, 2)), pltpu.SemaphoreType.DMA((8,)),
+            pltpu.SemaphoreType.DMA((2,)), pltpu.SemaphoreType.DMA((2,)),
             pltpu.SemaphoreType.DMA((2,)), pltpu.SemaphoreType.DMA((2,)),
             pltpu.SemaphoreType.DMA((2,)), pltpu.SemaphoreType.DMA((2,)),
             pltpu.SemaphoreType.DMA, pltpu.SemaphoreType.DMA,
@@ -349,13 +434,6 @@
             collective_id=0, has_side_effects=True, vmem_limit_bytes=60 * 2**20
         ),
     )(query_vectors, key_vectors, value_vectors, send_slots, receive_slots, resets)
-    return pl.pallas_call(
-        scale_rows,
-        name="scale",
-        out_shape=jax.ShapeDtypeStruct((TOK, WIDE), BF16),
-        in_specs=[vmem, vmem],
-        out_specs=vmem,
-    )(back, scale)
 
 
 def solution(mesh):

time: 107 us -> 98.6 us (0.921)
  Pallas kernels: 107 us -> 97.5 us
    pallas_call x2 -> x1, Pallas kernels: 107 us -> 97.5 us  [shards(): pl.pallas_call(kernel, name='attention', out_shape=pltpu.VMEM((TOK, WIDE)...]
where the time goes in v3:
time: 98.6 us; the launch traced here: 98.4 us
  Pallas kernels  97.5 us (99%)
    pallas_call x1, Pallas kernels, shards(): pl.pallas_call(kernel, name='attention', out_shape=pltpu.VMEM((TOK, WIDE)...  97.5 us

profile of v3, /device:TPU:1, one launch (start us, length us, event | category | flops | bytes accessed | tf_op | source)
XLA Modules:
  0.0 98.4 jit_solution(10368354991709989046)
XLA Ops:
  0.0 97.5 %attention.1 = bf16[1024,512]{1,0:T(8,128)(2,1)S(1)} custom-call(bf16[1024,512]{1,0:T(8,128)(2,1)} %q_hbm.1, bf16[1024,512]{1,0:T(8,128)(2,1)} %k_hbm.1, bf16[1024,512]{1,0:T(8,128)(2,1)} %v_hbm.1, s32[32,48]{1,0:T(8,128)} %send_ref.1, s32[32,48]{1,0:T(8,128)} %receive_ref.1, s32[8]{0:T(128)} %resets_ref.1), custom_call_target="tpu_custom_call" | custom-call | tf_op jit(solution)/shard_map/attention/pallas_call | solution.py:409
  97.5 1.0 copy.8

commit v4 on v3

--- a/solution.py
+++ b/solution.py
@@ -33,7 +33,7 @@
     q_hbm, k_hbm, v_hbm, send_ref, receive_ref, resets_ref, out_ref,
     q_ref, k_ref, v_ref, columns,
     pack_send, place_send, pack_recv, place_recv,
-    outbox, inbox, q_ctx, k_ctx, v_ctx, raw, late_raw, kv, carried,
+    outbox, inbox, q_ctx, k_ctx, v_ctx, raw, kv, carried,
     state_out, state_in, prefix_out, prefix_in, keeps, scale_out, scale_in, scale_parts, partial, z_box,
     in_sem, bulk_ssem, bulk_rsem, st_ssem, st_rsem, pf_ssem, pf_rsem, row_ssem, row_rsem, z_ssem, z_rsem,
 ):
@@ -247,10 +247,7 @@
                 value = jnp.dot(q, carried[half, c, h * HD : (h + 1) * HD, :], preferred_element_type=F32)
                 value = value + jnp.dot(weights, v_ctx[rows, cols], preferred_element_type=F32)
                 squares = squares + value * value
-                if half == 0:
-                    raw[rows, cols] = value.astype(BF16)
-                else:
-                    late_raw[rows, h * HD : (h + 1) * HD] = value
+                raw[rows, cols] = value.astype(BF16)
             row = to_row(jnp.sum(squares, axis=1, keepdims=True))
             if half == 0:
                 partial[c : c + 1, :] = row
@@ -261,12 +258,11 @@
         lax.broadcasted_iota(jnp.int32, (CAP, 128), 0) == lax.broadcasted_iota(jnp.int32, (CAP, 128), 1)
     )
 
-    def normalize(scale):
+    def split_scale(scale):
         lane = lax.broadcasted_iota(jnp.int32, (128, 128), 1)
         for c in range(TOK // 128):
             rows = slice(c * 128, (c + 1) * 128)
             column = to_column(scale[c : c + 1, :])
-            raw[rows, COLS:] = (late_raw[rows, :] * column).astype(BF16)
             rest = jnp.broadcast_to(column, (128, 128))
             parts = jnp.zeros((128, 128), F32)
             for i in range(3):
@@ -287,12 +283,16 @@
             scale_out[d] = jnp.sum(jnp.where(slots, spread, 0.0), axis=0, keepdims=True)
         scale_in[me] = scale_out[me]
 
-    def scale_arrived():
-        for s in range(N_SEQ):
-            rows = slice(s * CAP, (s + 1) * CAP)
-            spread = jnp.broadcast_to(scale_in[s], (CAP, 128))
-            column = jnp.sum(jnp.where(slots, spread, 0.0), axis=1, keepdims=True)
-            inbox[R0, rows, :] = (inbox[R0, rows, :].astype(F32) * column).astype(BF16)
+    def scales_to_columns():
+        for d in range(N_SEQ):
+            spread = jnp.broadcast_to(scale_in[d], (CAP, 128))
+            columns[d * CAP : (d + 1) * CAP, :] = jnp.sum(jnp.where(slots, spread, 0.0), axis=1, keepdims=True)
+
+    def scale_rows(stage):
+        @pl.loop(0, SLOTS // 384)
+        def _(i):
+            here = pl.ds(pl.multiple_of(i * 384, 384), 384)
+            inbox[stage, here, :] = (inbox[stage, here, :].astype(F32) * columns[here, :]).astype(BF16)
 
     keep_all = jnp.float32(1.0)
     for c in range(GROUPS):
@@ -373,20 +373,23 @@
         device_id_type=MESH,
     )
     send_bulk(R0, (1,))
+    pack_rows(pack_recv, raw, 1, R1)
+    send_bulk(R1, (0,))
     all_z.wait_recv()
     squares = z_box[0]
     for z in range(1, N_HEAD):
         squares = squares + z_box[z]
-    normalize(lax.rsqrt(squares / (H * HD) + epsilon))
+    split_scale(lax.rsqrt(squares / (H * HD) + epsilon))
     pack_scales()
     send_rows(lambda peer: scale_out.at[peer], scale_in, 1)
-    pack_rows(pack_recv, raw, 1, R1)
-    send_bulk(R1)
+    send_bulk(R1, (1,))
     arrived(R0)
     all_rows(scale_in, 1).wait_recv()
-    scale_arrived()
+    scales_to_columns()
+    scale_rows(R0)
     place_rows(place_send, R0, out_ref, 0)
     arrived(R1)
+    scale_rows(R1)
     place_rows(place_send, R1, out_ref, 1)
 
     all_z.wait_send()
@@ -417,7 +420,6 @@
             square(SLOTS, TOK), square(TOK, SLOTS), square(SLOTS, TOK), square(TOK, SLOTS),
             pltpu.VMEM((8, SLOTS, COLS), BF16), pltpu.VMEM((8, SLOTS, COLS), BF16),
             square(TOK, WIDE), square(TOK, WIDE), square(TOK, WIDE), square(TOK, WIDE),
-            pltpu.VMEM((TOK, COLS), F32),
             pltpu.VMEM((2, GROUPS, COLS, HD), F32), pltpu.VMEM((2, GROUPS, COLS, HD), BF16),
             pltpu.VMEM((2, N_SEQ, PIECE, HD), F32), pltpu.VMEM((2, N_SEQ, PIECE, HD), F32),
             pltpu.VMEM((2, N_SEQ, PIECE, HD), F32), pltpu.VMEM((2, N_SEQ, PIECE, HD), F32),

time: 98.6 us -> 93.9 us (0.952)
  Pallas kernels: 97.5 us -> 92.8 us
    pallas_call x1, Pallas kernels: 97.5 us -> 92.8 us  [shards(): pl.pallas_call(kernel, name='attention', out_shape=pltpu.VMEM((TOK, WIDE)...]
where the time goes in v4:
time: 93.9 us; the launch traced here: 93.8 us
  Pallas kernels  92.8 us (99%)
  local copies, waits for them, and re-layouts  0.97 us (1%)
    pallas_call x1, Pallas kernels, shards(): pl.pallas_call(kernel, name='attention', out_shape=pltpu.VMEM((TOK, WIDE)...  92.8 us

profile of v4, /device:TPU:1, one launch (start us, length us, event | category | flops | bytes accessed | tf_op | source)
XLA Modules:
  0.0 93.8 jit_solution(15965044220444789402)
XLA Ops:
  0.0 92.8 %attention.1 = bf16[1024,512]{1,0:T(8,128)(2,1)S(1)} custom-call(bf16[1024,512]{1,0:T(8,128)(2,1)} %q_hbm.1, bf16[1024,512]{1,0:T(8,128)(2,1)} %k_hbm.1, bf16[1024,512]{1,0:T(8,128)(2,1)} %v_hbm.1, s32[32,48]{1,0:T(8,128)} %send_ref.1, s32[32,48]{1,0:T(8,128)} %receive_ref.1, s32[8]{0:T(128)} %resets_ref.1), custom_call_target="tpu_custom_call" | custom-call | tf_op jit(solution)/shard_map/attention/pallas_call | solution.py:412
  92.8 1.0 %copy.8 = bf16[1024,512]{1,0:T(8,128)(2,1)} copy(bf16[1024,512]{1,0:T(8,128)(2,1)S(1)} %attention.1) | data formatting | bytes 2097152

commit v5 on v4

--- a/solution.py
+++ b/solution.py
@@ -34,7 +34,7 @@
     q_ref, k_ref, v_ref, columns,
     pack_send, place_send, pack_recv, place_recv,
     outbox, inbox, q_ctx, k_ctx, v_ctx, raw, kv, carried,
-    state_out, state_in, prefix_out, prefix_in, keeps, scale_out, scale_in, scale_parts, partial, z_box,
+    state_out, state_in, prefix_out, prefix_in, keeps, scale_out, scale_in, scale_parts, slot_parts, partial, z_box,
     in_sem, bulk_ssem, bulk_rsem, st_ssem, st_rsem, pf_ssem, pf_rsem, row_ssem, row_rsem, z_ssem, z_rsem,
 ):
     me = lax.axis_index("seq")
@@ -258,18 +258,19 @@
         lax.broadcasted_iota(jnp.int32, (CAP, 128), 0) == lax.broadcasted_iota(jnp.int32, (CAP, 128), 1)
     )
 
+    def three_terms(column, rows):
+        lane = lax.broadcasted_iota(jnp.int32, (rows, 128), 1)
+        rest = jnp.broadcast_to(column, (rows, 128))
+        parts = jnp.zeros((rows, 128), F32)
+        for i in range(3):
+            term = rest.astype(BF16).astype(F32)
+            parts = jnp.where(lane == i, term, parts)
+            rest = rest - term
+        return parts.astype(BF16)
+
     def split_scale(scale):
-        lane = lax.broadcasted_iota(jnp.int32, (128, 128), 1)
         for c in range(TOK // 128):
-            rows = slice(c * 128, (c + 1) * 128)
-            column = to_column(scale[c : c + 1, :])
-            rest = jnp.broadcast_to(column, (128, 128))
-            parts = jnp.zeros((128, 128), F32)
-            for i in range(3):
-                term = rest.astype(BF16).astype(F32)
-                parts = jnp.where(lane == i, term, parts)
-                rest = rest - term
-            scale_parts[rows, :] = parts.astype(BF16)
+            scale_parts[c * 128 : (c + 1) * 128, :] = three_terms(to_column(scale[c : c + 1, :]), 128)
 
     def pack_scales():
         @pl.loop(0, SLOTS // 384)
@@ -283,16 +284,24 @@
             scale_out[d] = jnp.sum(jnp.where(slots, spread, 0.0), axis=0, keepdims=True)
         scale_in[me] = scale_out[me]
 
-    def scales_to_columns():
+    def place_scales():
         for d in range(N_SEQ):
             spread = jnp.broadcast_to(scale_in[d], (CAP, 128))
-            columns[d * CAP : (d + 1) * CAP, :] = jnp.sum(jnp.where(slots, spread, 0.0), axis=1, keepdims=True)
-
-    def scale_rows(stage):
-        @pl.loop(0, SLOTS // 384)
+            column = jnp.sum(jnp.where(slots, spread, 0.0), axis=1, keepdims=True)
+            slot_parts[d * CAP : (d + 1) * CAP, :] = three_terms(column, CAP)
+
+        @pl.loop(0, TOK // 256)
         def _(i):
-            here = pl.ds(pl.multiple_of(i * 384, 384), 384)
-            inbox[stage, here, :] = (inbox[stage, here, :].astype(F32) * columns[here, :]).astype(BF16)
+            here = pl.ds(pl.multiple_of(i * 256, 256), 256)
+            parts = jnp.dot(place_send[here, :], slot_parts[...], preferred_element_type=F32)
+            columns[here, :] = jnp.sum(parts, axis=1, keepdims=True)
+
+    def place_scaled(stage, half):
+        @pl.loop(0, TOK // 256)
+        def _(i):
+            here = pl.ds(pl.multiple_of(i * 256, 256), 256)
+            rows = jnp.dot(place_send[here, :], inbox[stage], preferred_element_type=F32)
+            out_ref[here, half * COLS : (half + 1) * COLS] = (rows * columns[here, :]).astype(BF16)
 
     keep_all = jnp.float32(1.0)
     for c in range(GROUPS):
@@ -385,12 +394,10 @@
     send_bulk(R1, (1,))
     arrived(R0)
     all_rows(scale_in, 1).wait_recv()
-    scales_to_columns()
-    scale_rows(R0)
-    place_rows(place_send, R0, out_ref, 0)
+    place_scales()
+    place_scaled(R0, 0)
     arrived(R1)
-    scale_rows(R1)
-    place_rows(place_send, R1, out_ref, 1)
+    place_scaled(R1, 1)
 
     all_z.wait_send()
     for stage in (K0, V0, Q1, R0, R1):
@@ -424,7 +431,7 @@
             pltpu.VMEM((2, N_SEQ, PIECE, HD), F32), pltpu.VMEM((2, N_SEQ, PIECE, HD), F32),
             pltpu.VMEM((2, N_SEQ, PIECE, HD), F32), pltpu.VMEM((2, N_SEQ, PIECE, HD), F32),
             row_of_each(), row_of_each(), row_of_each(),
-            square(TOK, 128), pltpu.VMEM((TOK // 128, 128), F32), pltpu.VMEM((N_HEAD, TOK // 128, 128), F32),
+            square(TOK, 128), square(SLOTS, 128), pltpu.VMEM((TOK // 128, 128), F32), pltpu.VMEM((N_HEAD, TOK // 128, 128), F32),
             pltpu.SemaphoreType.DMA((3,)),
             pltpu.SemaphoreType.DMA((8, 2)), pltpu.SemaphoreType.DMA((8,)),
             pltpu.SemaphoreType.DMA((2,)), pltpu.SemaphoreType.DMA((2,)),

time: 93.9 us -> 93.8 us (level)
  no operation moved by 1% of the time
where the time goes in v5:
time: 93.8 us; the launch traced here: 93.6 us
  Pallas kernels  92.6 us (99%)
  local copies, waits for them, and re-layouts  0.97 us (1%)
    pallas_call x1, Pallas kernels, shards(): pl.pallas_call(kernel, name='attention', out_shape=pltpu.VMEM((TOK, WIDE)...  92.6 us

profile of v5, /device:TPU:1, one launch (start us, length us, event | category | flops | bytes accessed | tf_op | source)
XLA Modules:
  0.0 93.6 jit_solution(14807513037115841215)
XLA Ops:
  0.0 92.6 %attention.1 = bf16[1024,512]{1,0:T(8,128)(2,1)S(1)} custom-call(bf16[1024,512]{1,0:T(8,128)(2,1)} %q_hbm.1, bf16[1024,512]{1,0:T(8,128)(2,1)} %k_hbm.1, bf16[1024,512]{1,0:T(8,128)(2,1)} %v_hbm.1, s32[32,48]{1,0:T(8,128)} %send_ref.1, s32[32,48]{1,0:T(8,128)} %receive_ref.1, s32[8]{0:T(128)} %resets_ref.1), custom_call_target="tpu_custom_call" | custom-call | tf_op jit(solution)/shard_map/attention/pallas_call | solution.py:419
  92.6 1.0 %copy.8 = bf16[1024,512]{1,0:T(8,128)(2,1)} copy(bf16[1024,512]{1,0:T(8,128)(2,1)S(1)} %attention.1) | data formatting | bytes 2097152

commit v6 on v5

--- a/solution.py
+++ b/solution.py
@@ -42,13 +42,13 @@
 
     barrier = pltpu.get_barrier_semaphore()
 
-    @pl.loop(1, N_SEQ)
+    @pl.loop(1, N_SEQ, unroll=True)
     def _(k):
         pl.semaphore_signal(
             barrier, inc=1, device_id={"seq": lax.rem(me + k, N_SEQ), "head": mine}, device_id_type=MESH
         )
 
-    @pl.loop(1, N_HEAD)
+    @pl.loop(1, N_HEAD, unroll=True)
     def _(k):
         pl.semaphore_signal(
             barrier, inc=1, device_id={"seq": me, "head": lax.rem(mine + k, N_HEAD)}, device_id_type=MESH
@@ -126,10 +126,10 @@
             return one
 
         if 0 in parts:
-            pl.loop(1, EARLY + 1)(send(0))
+            pl.loop(1, EARLY + 1, unroll=True)(send(0))
             inbox[stage, block(me), :] = outbox[stage, block(me), :]
         if 1 in parts:
-            pl.loop(EARLY + 1, N_SEQ)(send(1))
+            pl.loop(EARLY + 1, N_SEQ, unroll=True)(send(1))
 
     def bulk_of(stage, blocks, part):
         rows = pl.ds(0, blocks * CAP)
@@ -152,7 +152,7 @@
         bulk_of(stage, N_SEQ - 1 - EARLY, 1).wait_send()
 
     def send_small(source, target, half, ssem, rsem):
-        @pl.loop(1, N_SEQ)
+        @pl.loop(1, N_SEQ, unroll=True)
         def _(k):
             peer = lax.rem(me + 13 * k, N_SEQ)
             pltpu.make_async_remote_copy(
@@ -177,7 +177,7 @@
         )
 
     def send_rows(source_of, target, which):
-        @pl.loop(1, N_SEQ)
+        @pl.loop(1, N_SEQ, unroll=True)
         def _(k):
             peer = lax.rem(me + 13 * k, N_SEQ)
             pltpu.make_async_remote_copy(
@@ -362,7 +362,7 @@
     all_small(prefix_out, prefix_in, 1, pf_ssem, pf_rsem).wait_recv()
     attend(1)
 
-    @pl.loop(1, N_HEAD)
+    @pl.loop(1, N_HEAD, unroll=True)
     def _(k):
         pltpu.make_async_remote_copy(
             src_ref=z_box.at[mine],

time: 93.8 us -> 92.9 us (level)
  no operation moved by 1% of the time
where the time goes in v6:
time: 92.9 us; the launch traced here: 92.8 us
  Pallas kernels  91.8 us (99%)
  local copies, waits for them, and re-layouts  0.97 us (1%)
    pallas_call x1, Pallas kernels, shards(): pl.pallas_call(kernel, name='attention', out_shape=pltpu.VMEM((TOK, WIDE)...  91.8 us

profile of v6, /device:TPU:1, one launch (start us, length us, event | category | flops | bytes accessed | tf_op | source)
XLA Modules:
  0.0 92.8 jit_solution(11398496591764026425)
XLA Ops:
  0.0 91.8 %attention.1 = bf16[1024,512]{1,0:T(8,128)(2,1)S(1)} custom-call(bf16[1024,512]{1,0:T(8,128)(2,1)} %q_hbm.1, bf16[1024,512]{1,0:T(8,128)(2,1)} %k_hbm.1, bf16[1024,512]{1,0:T(8,128)(2,1)} %v_hbm.1, s32[32,48]{1,0:T(8,128)} %send_ref.1, s32[32,48]{1,0:T(8,128)} %receive_ref.1, s32[8]{0:T(128)} %resets_ref.1), custom_call_target="tpu_custom_call" | custom-call | tf_op jit(solution)/shard_map/attention/pallas_call | solution.py:419
  91.8 1.0 %copy.8 = bf16[1024,512]{1,0:T(8,128)(2,1)} copy(bf16[1024,512]{1,0:T(8,128)(2,1)S(1)} %attention.1) | data formatting | bytes 2097152

commit v7 on v6

--- a/solution.py
+++ b/solution.py
@@ -100,7 +100,7 @@
             ).astype(BF16)
 
     def place_rows(place, stage, rows_ref, half):
-        @pl.loop(0, TOK // 256)
+        @pl.loop(0, TOK // 256, unroll=True)
         def _(i):
             here = pl.ds(pl.multiple_of(i * 256, 256), 256)
             rows_ref[here, half * COLS : (half + 1) * COLS] = jnp.dot(
@@ -297,7 +297,7 @@
             columns[here, :] = jnp.sum(parts, axis=1, keepdims=True)
 
     def place_scaled(stage, half):
-        @pl.loop(0, TOK // 256)
+        @pl.loop(0, TOK // 256, unroll=True)
         def _(i):
             here = pl.ds(pl.multiple_of(i * 256, 256), 256)
             rows = jnp.dot(place_send[here, :], inbox[stage], preferred_element_type=F32)

time: 92.9 us -> 92.6 us (level)
  no operation moved by 1% of the time
where the time goes in v7:
time: 92.6 us; the launch traced here: 92.4 us
  Pallas kernels  91.5 us (99%)
  local copies, waits for them, and re-layouts  0.97 us (1%)
    pallas_call x1, Pallas kernels, shards(): pl.pallas_call(kernel, name='attention', out_shape=pltpu.VMEM((TOK, WIDE)...  91.5 us

profile of v7, /device:TPU:1, one launch (start us, length us, event | category | flops | bytes accessed | tf_op | source)
XLA Modules:
  0.0 92.4 jit_solution(10063736073023647597)
XLA Ops:
  0.0 91.5 %attention.1 = bf16[1024,512]{1,0:T(8,128)(2,1)S(1)} custom-call(bf16[1024,512]{1,0:T(8,128)(2,1)} %q_hbm.1, bf16[1024,512]{1,0:T(8,128)(2,1)} %k_hbm.1, bf16[1024,512]{1,0:T(8,128)(2,1)} %v_hbm.1, s32[32,48]{1,0:T(8,128)} %send_ref.1, s32[32,48]{1,0:T(8,128)} %receive_ref.1, s32[8]{0:T(128)} %resets_ref.1), custom_call_target="tpu_custom_call" | custom-call | tf_op jit(solution)/shard_map/attention/pallas_call | solution.py:419
  91.5 1.0 %copy.8 = bf16[1024,512]{1,0:T(8,128)(2,1)} copy(bf16[1024,512]{1,0:T(8,128)(2,1)S(1)} %attention.1) | data formatting | bytes 2097152
